TPU v7x, 32 devices: a whole 2x2x4 slice. The times are simulated.
32 devices in a mesh: grp: 2 (over x), wide: 16 (over z, y, core).
Axes of the slice: x: 2, y: 2, z: 4, core: 2. Of those that a mesh axis runs over, the one named last changes fastest.
Arguments:
- slab: float32 [6, 2, 4096, 4096], P('grp', None, None, 'wide'), parts along dimension 0, may hold values from -6 to 6
- factor: float32 [4096, 256], P('wide'), may hold values from -0.09375 to 0.09375
Outputs:
- gram: float32 [8192, 4096], P(('grp', 'wide')), parts along dimension 0
There are 2 independent parts, one for each index of `grp`. A program takes and returns all parts, laid end to end along the dimension named above; an argument that names none is the same for every part. Nothing has to cross between parts.
All inputs are finite; a program needn't handle non-finite values.
Results may differ from a plain program's by a relative error of at most 0.0034.
Values may be sent and summed in bfloat16 or wider, within the bound.
A program may use at most 128 MiB of HBM per device.

v0:
```python
import jax
import jax.numpy as jnp
from jax import lax
from jax.sharding import PartitionSpec as P


def shards(slab, factor):
    count_rows = slab.shape[2] // lax.axis_size("wide")
    term = jnp.einsum("pvin,nr->ipvr", slab, factor, precision=lax.Precision.HIGHEST)
    summed = lax.psum_scatter(
        term.reshape(count_rows * lax.axis_size("wide"), -1),
        "wide",
        scatter_dimension=0,
        tiled=True,
    )
    projected = summed.astype(jnp.bfloat16)
    width = projected.shape[1]
    gram = lax.dot_general(
        projected,
        lax.all_gather(projected, "wide", axis=0, tiled=True),
        (((1,), (1,)), ((), ())),
        preferred_element_type=jnp.float32,
    )
    return gram / float(width)


def solution(mesh):
    placed = (P("grp", None, None, "wide"), P("wide", None))
    return jax.shard_map(
        shards, mesh=mesh, in_specs=placed, out_specs=P(("grp", "wide"), None), check_vma=False
    )
```

profile of v0, /device:TPU:0, one launch (start us, length us, event | category | flops | bytes accessed | tf_op | source)
XLA Modules:
  0.0 423.6 jit_solution(6554191025420923892)
XLA Ops:
  6.5 0.0 copy-start
  6.5 0.0 reduce-scatter.2.cloned.1.call-start
  6.5 0.9 copy-done
  7.5 46.4 %fusion = f32[256,3,2,4096]{3,0,2,1:T(8,128)} fusion(f32[3,2,4096,256]{3,2,1,0:T(8,128)} %param.2, f32[256,256]{1,0:T(8,128)S(1)} %copy-done), kind=kOutput, calls=%fused_computation.1 | convolution fusion | flops 19327352832 | bytes 50593792 | tf_op jit(solution)/shard_map/pvin,nr->ipvr/dot_general | solution.py:9
  53.9 0.0 reduce-scatter.2.cloned.1.call-update
  53.9 0.0 copy-start.1
  53.9 0.0 all-gather.2.cloned.1.call-start
  53.9 246.7 %reduce-scatter.2.cloned.1.call-done = f32[256,1536]{0,1:T(8,128)} async-done(((f32[4096,1536]{0,1:T(8,128)}), f32[256,1536]{0,1:T(8,128)}) %reduce-scatter.2.cloned.1.call-update) | async-done | bytes 1572880 | tf_op jit(solution)/shard_map/reduce_scatter | solution.py:10
  300.6 2.4 convert_element_type.3
  303.1 0.0 all-gather.2.cloned.1.call-update
  303.1 103.2 %all-gather.2.cloned.1.call-done = bf16[4096,1536]{0,1:T(8,128)(2,1)} async-done(((bf16[256,1536]{0,1:T(8,128)(2,1)}), bf16[4096,1536]{0,1:T(8,128)(2,1)}) %all-gather.2.cloned.1.call-update) | async-done | bytes 12582928 | tf_op jit(solution)/shard_map/all_gather | solution.py:20
  406.3 10.4 %convolution_multiply_fusion = f32[256,4096]{1,0:T(8,128)} fusion(bf16[256,1536]{0,1:T(8,128)(2,1)} %convert_element_type.3, bf16[4096,1536]{0,1:T(8,128)(2,1)} %all-gather.2.cloned.1.call-done), kind=kOutput, calls=%fused_computation | convolution fusion | flops 3222274048 | bytes 17563648 | tf_op jit(solution)/shard_map/dot_general | solution.py:18
  416.7 0.0 copy-done.1
Async XLA Ops:
  6.5 1.0 copy-start
  6.5 294.1 %reduce-scatter.2.cloned.1.call-start = ((), (), s32[]{:S(2)}) async-start(), calls=%async_computation.1 | async-start | bytes 26738688 | tf_op jit(solution)/shard_map/reduce_scatter | solution.py:10
  53.9 362.8 %copy-start.1 = (f32[256,256]{1,0:T(8,128)S(1)}, f32[256,256]{1,0:T(8,128)}, u32[]{:S(2)}) copy-start(f32[256,256]{1,0:T(8,128)} %param.3) | copy-start | bytes 786436
  53.9 352.4 %all-gather.2.cloned.1.call-start = ((), (), s32[]{:S(2)}) async-start(), calls=%async_computation.2 | async-start | bytes 13369344 | tf_op jit(solution)/shard_map/all_gather | solution.py:20
Sparse Core Ops, SparseCore 0:
  54.0 246.6 reduce-scatter.1
  303.2 103.0 all-gather.1
where the time goes:
time: 424 us
  waiting for transfers between devices  350 us (83%)
  matrix products  56.8 us (13%)
  between operations  13.4 us (3%)
    reduce_scatter x1, waiting for transfers between devices, shards(): lax.psum_scatter(term.reshape(count_rows * lax.axis_size('wide'), -1), 'w...  247 us
    all_gather x1, waiting for transfers between devices, shards(): lax.all_gather(projected, 'wide', axis=0, tiled=True)  103 us
    dot_general x1, matrix products, shards(): jnp.einsum('pvin,nr->ipvr', slab, factor, precision=lax.Precision.HIGHEST)  46.4 us
    dot_general x1, matrix products, shards(): lax.dot_general(projected, lax.all_gather(projected, 'wide', axis=0, tile...  10.4 us
  transfers between devices with their start and end apart: 2, of which 2 were waited for; matrix products, arithmetic and copies ran while one was open for 0% of the time, Pallas kernels for 0%

commit v1 on v0

v1 whole, which is shorter than its diff:
```python
import functools

import jax
import jax.numpy as jnp
from jax import lax
from jax.experimental import pallas as pl
from jax.experimental.pallas import tpu as pltpu
from jax.sharding import PartitionSpec as P

HALVES = 2


def narrow_hops(chips):
    hops = 0
    while 8 * (hops + 1) * (hops + 2) // 2 <= 3 * chips:
        hops += 1
    return hops


def kernel(
    chips, lanes, narrow, scale,
    slab, factor, gram,
    fsplit, fields, stage, sib, ring, narrow_out, narrow_in, held, gram_out, gram_in,
    field_sem, sib_send, sib_recv, hop_send, hop_recv, gather_send, gather_recv, gram_send, gram_recv,
):
    own_planes, rows = ring.shape[1], ring.shape[2]
    part = rows // HALVES
    me = lax.axis_index("wide")
    chip, core = lax.div(me, HALVES), lax.rem(me, HALVES)
    way = 1 - 2 * core

    def wrap(place):
        return lax.rem(place + 2 * chips, chips)

    def chip_at(place):
        if lanes == 1:
            return place
        lane = lax.div(place, chips // 2)
        return 2 * (place + lane * (chips - 1 - 2 * place)) + lane

    if lanes == 1:
        place = chip
    else:
        level, lane = lax.div(chip, 2), lax.rem(chip, 2)
        place = level + lane * (chips - 1 - 2 * level)

    after = {"wide": chip_at(wrap(place + way)) * HALVES + core}
    before = {"wide": chip_at(wrap(place - way)) * HALVES + core}
    sibling = {"wide": chip * HALVES + 1 - core}

    def fetch(step, which):
        towards = way if which == 0 else -way
        half = core if which == 0 else 1 - core
        first = pl.multiple_of(chip_at(wrap(place - towards * (1 + step))) * rows, rows)
        slot = lax.rem(step, 2)
        return pltpu.make_async_copy(
            slab.at[pl.ds(half * own_planes, own_planes), pl.ds(first, rows), :],
            fields.at[slot, which],
            field_sem.at[slot, which],
        )

    def remote(src, dst, send, recv, to):
        return pltpu.make_async_remote_copy(
            src_ref=src, dst_ref=dst, send_sem=send, recv_sem=recv,
            device_id=to, device_id_type=pl.DeviceIdType.MESH,
        )

    def to_sibling(step, j):
        slot = lax.rem(step, 2)
        return remote(stage.at[slot, j], sib.at[step, j], sib_send.at[slot, j], sib_recv.at[step, j], sibling)

    def wide_hop(step, j):
        return remote(ring.at[step - narrow, j], ring.at[step + 1 - narrow, j],
                      hop_send.at[step, j], hop_recv.at[step, j], after)

    def narrow_hop(step, j):
        return remote(narrow_out.at[step, j], narrow_in.at[step, j],
                      hop_send.at[step, j], hop_recv.at[step, j], after)

    def gather_hop(step, j):
        chunk = wrap(place - way * step)
        return remote(held.at[chunk, j], held.at[chunk, j],
                      gather_send.at[step, j], gather_recv.at[step, j], after)

    def gather_arrival(step, j):
        chunk = wrap(place - way * (step + 1))
        return remote(held.at[chunk, j], held.at[chunk, j],
                      gather_send.at[step, j], gather_recv.at[step, j], after)

    def gram_part(chunk):
        return remote(gram_out.at[chunk], gram_in.at[chunk], gram_send.at[chunk], gram_recv.at[chunk], sibling)

    def term(slot, which, j):
        x = fields[slot, which, j]
        high = x.astype(jnp.bfloat16)
        low = (x - high.astype(jnp.float32)).astype(jnp.bfloat16)
        dot = functools.partial(jnp.dot, preferred_element_type=jnp.float32)
        return dot(high, fsplit[0]) + (dot(high, fsplit[1]) + dot(low, fsplit[0]))

    def relay(step, reuse):
        fetch(step, 1).wait()
        slot = lax.rem(step, 2)

        def one(j, _):
            if reuse:
                to_sibling(step - 2, j).wait_send()
            stage[slot, j] = term(slot, 1, j)
            to_sibling(step, j).start()
            return _

        lax.fori_loop(0, own_planes, one, 0)

    def combine(step, kind_in, kind_out):
        fetch(step, 0).wait()
        slot = lax.rem(step, 2)

        def one(j, _):
            value = term(slot, 0, j)
            to_sibling(step, j).wait_recv()
            value = value + sib[step, j]
            if kind_in == "narrow":
                narrow_hop(step - 1, j).wait_recv()
                value = value + narrow_in[step - 1, j].astype(jnp.float32)
            elif kind_in == "wide":
                wide_hop(step - 1, j).wait_recv()
                value = value + ring[step - narrow, j]
            if kind_out == "narrow":
                narrow_out[step, j] = value.astype(jnp.bfloat16)
                narrow_hop(step, j).start()
            elif kind_out == "wide":
                ring[step - narrow, j] = value
                wide_hop(step, j).start()
            else:
                held[place, j] = value.astype(jnp.bfloat16)
                gather_hop(0, j).start()
            return _

        lax.fori_loop(0, own_planes, one, 0)

    def multiply(chunk):
        def rows_of(half):
            first = pl.multiple_of(half * part, part)
            total = None
            for j in range(own_planes):
                product = lax.dot_general(
                    held[place, j, pl.ds(first, part), :], held[chunk, j],
                    (((1,), (1,)), ((), ())), preferred_element_type=jnp.float32,
                )
                total = product if total is None else total + product
            return total

        gram_out[chunk] = rows_of(1 - core)
        gram_part(chunk).start()
        columns = pl.ds(pl.multiple_of(chip_at(chunk) * rows, rows), rows)
        gram[:, columns] = rows_of(core)

    for step in range(2):
        fetch(step, 1).start()
        fetch(step, 0).start()
    f = factor[...]
    fsplit[0] = f.astype(jnp.bfloat16)
    fsplit[1] = (f - f.astype(jnp.bfloat16).astype(jnp.float32)).astype(jnp.bfloat16)

    barrier = pltpu.get_barrier_semaphore()
    for other in (after, before, sibling):
        pl.semaphore_signal(barrier, inc=1, device_id=other, device_id_type=pl.DeviceIdType.MESH)
    pl.semaphore_wait(barrier, 3)

    relay(0, False)
    for step in range(narrow + 1):
        kind_in = None if step == 0 else "narrow"
        combine(step, kind_in, "narrow" if step < narrow else "wide")
        relay(step + 1, step + 1 >= 2)
        fetch(step + 2, 1).start()
        fetch(step + 2, 0).start()

    def middle(step, _):
        combine(step, "wide", "wide")
        relay(step + 1, True)

        @pl.when(step + 2 < chips)
        def _fetch():
            fetch(step + 2, 1).start()
            fetch(step + 2, 0).start()

        return _

    lax.fori_loop(narrow + 1, chips - 1, middle, 0)
    combine(chips - 1, "wide", "held")
    multiply(place)

    def gathered(step, _):
        def one(j, _):
            gather_arrival(step - 1, j).wait_recv()

            @pl.when(step < chips - 1)
            def _pass_on():
                gather_hop(step, j).start()

            return _

        lax.fori_loop(0, own_planes, one, 0)
        multiply(wrap(place - way * step))
        return _

    lax.fori_loop(1, chips, gathered, 0)

    def finish(chunk, _):
        gram_part(chunk).wait()
        columns = pl.ds(pl.multiple_of(chip_at(chunk) * rows, rows), rows)
        gram[:, columns] = (gram[:, columns] + gram_in[chunk]) * scale
        return _

    lax.fori_loop(0, chips, finish, 0)

    def drain(j, _):
        to_sibling(chips - 2, j).wait_send()
        to_sibling(chips - 1, j).wait_send()
        for step in range(narrow):
            narrow_hop(step, j).wait_send()

        def hop(step, _):
            wide_hop(step, j).wait_send()
            return _

        lax.fori_loop(narrow, chips - 1, hop, 0)

        def gather(step, _):
            gather_hop(step, j).wait_send()
            return _

        lax.fori_loop(0, chips - 1, gather, 0)
        return _

    lax.fori_loop(0, own_planes, drain, 0)


def shards(lanes, slab, factor):
    planes = slab.shape[0] * slab.shape[1]
    total_rows, depth = slab.shape[2:]
    ranks = factor.shape[1]
    devices = lax.axis_size("wide")
    chips = devices // HALVES
    rows = total_rows // chips
    own = planes // HALVES
    narrow = narrow_hops(chips)
    f32, bf16 = jnp.float32, jnp.bfloat16
    block = (own, rows, ranks)
    dma = pltpu.SemaphoreType.DMA
    return pl.pallas_call(
        functools.partial(kernel, chips, lanes, narrow, 1.0 / float(planes * ranks)),
        out_shape=jax.ShapeDtypeStruct((total_rows // devices, total_rows), f32),
        in_specs=[pl.BlockSpec(memory_space=pl.ANY), pl.BlockSpec(memory_space=pltpu.VMEM)],
        out_specs=pl.BlockSpec(memory_space=pltpu.VMEM),
        scratch_shapes=[
            pltpu.VMEM((2, depth, ranks), bf16),
            pltpu.VMEM((2, 2, own, rows, depth), f32),
            pltpu.VMEM((2,) + block, f32),
            pltpu.VMEM((chips,) + block, f32),
            pltpu.VMEM((chips - narrow,) + block, f32),
            pltpu.VMEM((max(narrow, 1),) + block, bf16),
            pltpu.VMEM((max(narrow, 1),) + block, bf16),
            pltpu.VMEM((chips,) + block, bf16),
            pltpu.VMEM((chips, rows // HALVES, rows), f32),
            pltpu.VMEM((chips, rows // HALVES, rows), f32),
            dma((2, 2)),
            dma((2, own)),
            dma((chips, own)),
            dma((chips - 1, own)),
            dma((chips - 1, own)),
            dma((chips - 1, own)),
            dma((chips - 1, own)),
            dma((chips,)),
            dma((chips,)),
        ],
        compiler_params=pltpu.CompilerParams(
            collective_id=0, has_side_effects=True, vmem_limit_bytes=60 * 2**20
        ),
        cost_estimate=pl.CostEstimate(
            flops=8 * planes * total_rows * depth * ranks, bytes_accessed=4 * slab.size, transcendentals=0
        ),
    )(slab.reshape(planes, total_rows, depth), factor)


def solution(mesh):
    lanes = 2 if mesh.shape["grp"] == 2 else 1
    placed = (P("grp", None, None, "wide"), P("wide", None))
    return jax.shard_map(
        functools.partial(shards, lanes),
        mesh=mesh, in_specs=placed, out_specs=P(("grp", "wide"), None), check_vma=False,
    )
```

time: 424 us -> 179 us (0.42)
  waiting for transfers between devices: 350 us -> 0 us
  Pallas kernels: 0 us -> 175 us
  matrix products: 56.8 us -> 0 us
  between operations: 13.4 us -> 0.01 us
    reduce_scatter x1 -> x0, waiting for transfers between devices: 247 us -> none  [shards(): lax.psum_scatter(term.reshape(count_rows * lax.axis_size('wide'), -1), 'w...]
    pallas_call x0 -> x1, Pallas kernels: none -> 175 us  [shards(): pl.pallas_call(functools.partial(kernel, chips, lanes, narrow, 1.0 / floa...]
    all_gather x1 -> x0, waiting for transfers between devices: 103 us -> none  [shards(): lax.all_gather(projected, 'wide', axis=0, tiled=True)]
    dot_general x2 -> x0, matrix products: 56.8 us -> none  [the longest x1 46.4 us: shards(): jnp.einsum('pvin,nr->ipvr', slab, factor, precision=lax.Precision.HIGHEST)]
  transfers between devices with their start and end apart: 2 -> 0, of which waited for: 2 -> 0; matrix products, arithmetic and copies ran while one was open for 0% -> 0% of each run, Pallas kernels for 0% -> 0%
where the time goes in v1:
time: 179 us
  Pallas kernels  175 us (98%)
  local copies, waits for them, and re-layouts  4.65 us (3%)
    pallas_call x1, Pallas kernels, shards(): pl.pallas_call(functools.partial(kernel, chips, lanes, narrow, 1.0 / floa...  175 us
    unnamed x1, local copies, waits for them, and re-layouts  4.65 us

profile of v1, /device:TPU:0, one launch (start us, length us, event | category | flops | bytes accessed | tf_op | source)
XLA Modules:
  0.0 179.3 jit_solution(12092049904240827025)
XLA Ops:
  0.0 174.6 %shard_map.28 = f32[256,4096]{1,0:T(8,128)} custom-call(f32[6,4096,256]{2,1,0:T(8,128)} %bitcast.1, f32[256,256]{1,0:T(8,128)} %factor.1), custom_call_target="tpu_custom_call" | custom-call | flops 12884901888 | bytes 25165824 | tf_op jit(solution)/shard_map/pallas_call | solution.py:250
  174.6 4.7 %copy.4 = f32[256,4096]{1,0:T(8,128)} copy(f32[256,4096]{1,0:T(8,128)} %shard_map.28) | data formatting | bytes 8388608

commit v2 on v1

--- a/solution.py
+++ b/solution.py
@@ -10,20 +10,31 @@
 HALVES = 2
 
 
-def narrow_hops(chips):
-    hops = 0
-    while 8 * (hops + 1) * (hops + 2) // 2 <= 3 * chips:
-        hops += 1
-    return hops
+SPAN = 83.0
+PEAK_ROWS = 16
+
+
+def encode(value, code):
+    rows = value.shape[0]
+    peak = jnp.maximum(jnp.max(jnp.abs(value), axis=0, keepdims=True), 1e-30).astype(jnp.bfloat16)
+    wide_peak = peak.astype(jnp.float32)
+    code[pl.ds(0, rows), :] = jnp.exp(value * (SPAN / wide_peak)).astype(jnp.bfloat16)
+    code[pl.ds(rows, PEAK_ROWS), :] = jnp.broadcast_to(wide_peak, (PEAK_ROWS, value.shape[1])).astype(jnp.bfloat16)
+
+
+def decode(code):
+    rows = code.shape[0] - PEAK_ROWS
+    peak = code[pl.ds(rows, PEAK_ROWS), :].astype(jnp.float32)[:1]
+    return jnp.log(code[pl.ds(0, rows), :].astype(jnp.float32)) * (peak / SPAN)
 
 
 def kernel(
-    chips, lanes, narrow, scale,
+    chips, lanes, scale,
     slab, factor, gram,
-    fsplit, fields, stage, sib, ring, narrow_out, narrow_in, held, gram_out, gram_in,
+    fsplit, fields, stage, sib, code_out, code_in, held, gram_out, gram_in,
     field_sem, sib_send, sib_recv, hop_send, hop_recv, gather_send, gather_recv, gram_send, gram_recv,
 ):
-    own_planes, rows = ring.shape[1], ring.shape[2]
+    own_planes, rows = sib.shape[1], sib.shape[2]
     part = rows // HALVES
     me = lax.axis_index("wide")
     chip, core = lax.div(me, HALVES), lax.rem(me, HALVES)
@@ -69,12 +80,8 @@
         slot = lax.rem(step, 2)
         return remote(stage.at[slot, j], sib.at[step, j], sib_send.at[slot, j], sib_recv.at[step, j], sibling)
 
-    def wide_hop(step, j):
-        return remote(ring.at[step - narrow, j], ring.at[step + 1 - narrow, j],
-                      hop_send.at[step, j], hop_recv.at[step, j], after)
-
-    def narrow_hop(step, j):
-        return remote(narrow_out.at[step, j], narrow_in.at[step, j],
+    def hop(step, j):
+        return remote(code_out.at[step, j], code_in.at[step, j],
                       hop_send.at[step, j], hop_recv.at[step, j], after)
 
     def gather_hop(step, j):
@@ -97,43 +104,31 @@
         dot = functools.partial(jnp.dot, preferred_element_type=jnp.float32)
         return dot(high, fsplit[0]) + (dot(high, fsplit[1]) + dot(low, fsplit[0]))
 
-    def relay(step, reuse):
-        fetch(step, 1).wait()
+    def relay(step, j, reuse):
         slot = lax.rem(step, 2)
-
-        def one(j, _):
-            if reuse:
-                to_sibling(step - 2, j).wait_send()
-            stage[slot, j] = term(slot, 1, j)
-            to_sibling(step, j).start()
-            return _
-
-        lax.fori_loop(0, own_planes, one, 0)
-
-    def combine(step, kind_in, kind_out):
-        fetch(step, 0).wait()
-        slot = lax.rem(step, 2)
-
-        def one(j, _):
-            value = term(slot, 0, j)
-            to_sibling(step, j).wait_recv()
-            value = value + sib[step, j]
-            if kind_in == "narrow":
-                narrow_hop(step - 1, j).wait_recv()
-                value = value + narrow_in[step - 1, j].astype(jnp.float32)
-            elif kind_in == "wide":
-                wide_hop(step - 1, j).wait_recv()
-                value = value + ring[step - narrow, j]
-            if kind_out == "narrow":
-                narrow_out[step, j] = value.astype(jnp.bfloat16)
-                narrow_hop(step, j).start()
-            elif kind_out == "wide":
-                ring[step - narrow, j] = value
-                wide_hop(step, j).start()
-            else:
-                held[place, j] = value.astype(jnp.bfloat16)
-                gather_hop(0, j).start()
-            return _
+        if reuse:
+            to_sibling(step - 2, j).wait_send()
+        stage[slot, j] = term(slot, 1, j)
+        to_sibling(step, j).start()
+
+    def combine(step, j, first, last):
+        value = term(lax.rem(step, 2), 0, j)
+        to_sibling(step, j).wait_recv()
+        value = value + sib[step, j]
+        if not first:
+            hop(step - 1, j).wait_recv()
+            value = value + decode(code_in.at[step - 1, j])
+        if last:
+            held[place, j] = value.astype(jnp.bfloat16)
+            gather_hop(0, j).start()
+        else:
+            encode(value, code_out.at[step, j])
+            hop(step, j).start()
+
+    def each(body):
+        def one(j, carry):
+            body(j)
+            return carry
 
         lax.fori_loop(0, own_planes, one, 0)
 
@@ -166,27 +161,34 @@
         pl.semaphore_signal(barrier, inc=1, device_id=other, device_id_type=pl.DeviceIdType.MESH)
     pl.semaphore_wait(barrier, 3)
 
-    relay(0, False)
-    for step in range(narrow + 1):
-        kind_in = None if step == 0 else "narrow"
-        combine(step, kind_in, "narrow" if step < narrow else "wide")
-        relay(step + 1, step + 1 >= 2)
-        fetch(step + 2, 1).start()
-        fetch(step + 2, 0).start()
-
-    def middle(step, _):
-        combine(step, "wide", "wide")
-        relay(step + 1, True)
+    fetch(0, 1).wait()
+    relay(0, 0, False)
+    fetch(0, 0).wait()
+    for j in range(own_planes):
+        if j + 1 < own_planes:
+            relay(0, j + 1, False)
+        combine(0, j, True, False)
+    fetch(2, 1).start()
+    fetch(2, 0).start()
+    fetch(1, 1).wait()
+    each(lambda j: relay(1, j, False))
+
+    def middle(step, carry):
+        fetch(step, 0).wait()
+        each(lambda j: combine(step, j, False, False))
 
         @pl.when(step + 2 < chips)
         def _fetch():
             fetch(step + 2, 1).start()
             fetch(step + 2, 0).start()
 
-        return _
-
-    lax.fori_loop(narrow + 1, chips - 1, middle, 0)
-    combine(chips - 1, "wide", "held")
+        fetch(step + 1, 1).wait()
+        each(lambda j: relay(step + 1, j, True))
+        return carry
+
+    lax.fori_loop(1, chips - 1, middle, 0)
+    fetch(chips - 1, 0).wait()
+    each(lambda j: combine(chips - 1, j, False, True))
     multiply(place)
 
     def gathered(step, _):
@@ -216,14 +218,12 @@
     def drain(j, _):
         to_sibling(chips - 2, j).wait_send()
         to_sibling(chips - 1, j).wait_send()
-        for step in range(narrow):
-            narrow_hop(step, j).wait_send()
-
-        def hop(step, _):
-            wide_hop(step, j).wait_send()
+
+        def sums(step, _):
+            hop(step, j).wait_send()
             return _
 
-        lax.fori_loop(narrow, chips - 1, hop, 0)
+        lax.fori_loop(0, chips - 1, sums, 0)
 
         def gather(step, _):
             gather_hop(step, j).wait_send()
@@ -243,12 +243,11 @@
     chips = devices // HALVES
     rows = total_rows // chips
     own = planes // HALVES
-    narrow = narrow_hops(chips)
     f32, bf16 = jnp.float32, jnp.bfloat16
     block = (own, rows, ranks)
     dma = pltpu.SemaphoreType.DMA
     return pl.pallas_call(
-        functools.partial(kernel, chips, lanes, narrow, 1.0 / float(planes * ranks)),
+        functools.partial(kernel, chips, lanes, 1.0 / float(planes * ranks)),
         out_shape=jax.ShapeDtypeStruct((total_rows // devices, total_rows), f32),
         in_specs=[pl.BlockSpec(memory_space=pl.ANY), pl.BlockSpec(memory_space=pltpu.VMEM)],
         out_specs=pl.BlockSpec(memory_space=pltpu.VMEM),
@@ -257,9 +256,8 @@
             pltpu.VMEM((2, 2, own, rows, depth), f32),
             pltpu.VMEM((2,) + block, f32),
             pltpu.VMEM((chips,) + block, f32),
-            pltpu.VMEM((chips - narrow,) + block, f32),
-            pltpu.VMEM((max(narrow, 1),) + block, bf16),
-            pltpu.VMEM((max(narrow, 1),) + block, bf16),
+            pltpu.VMEM((chips - 1, own, rows + PEAK_ROWS, ranks), bf16),
+            pltpu.VMEM((chips - 1, own, rows + PEAK_ROWS, ranks), bf16),
             pltpu.VMEM((chips,) + block, bf16),
             pltpu.VMEM((chips, rows // HALVES, rows), f32),
             pltpu.VMEM((chips, rows // HALVES, rows), f32),

time: 179 us -> 139 us (0.78)
  Pallas kernels: 175 us -> 135 us
    pallas_call x1, Pallas kernels: 175 us -> 135 us  [shards(): pl.pallas_call(functools.partial(kernel, chips, lanes, 1.0 / float(planes...]
where the time goes in v2:
time: 139 us
  Pallas kernels  135 us (97%)
  local copies, waits for them, and re-layouts  4.65 us (3%)
    pallas_call x1, Pallas kernels, shards(): pl.pallas_call(functools.partial(kernel, chips, lanes, 1.0 / float(planes...  135 us
    unnamed x1, local copies, waits for them, and re-layouts  4.65 us

profile of v2, /device:TPU:0, one launch (start us, length us, event | category | flops | bytes accessed | tf_op | source)
XLA Modules:
  0.0 139.3 jit_solution(10971485040430808612)
XLA Ops:
  0.0 134.6 %shard_map.28 = f32[256,4096]{1,0:T(8,128)} custom-call(f32[6,4096,256]{2,1,0:T(8,128)} %bitcast.1, f32[256,256]{1,0:T(8,128)} %factor.1), custom_call_target="tpu_custom_call" | custom-call | flops 12884901888 | bytes 25165824 | tf_op jit(solution)/shard_map/pallas_call | solution.py:249
  134.6 4.7 %copy.4 = f32[256,4096]{1,0:T(8,128)} copy(f32[256,4096]{1,0:T(8,128)} %shard_map.28) | data formatting | bytes 8388608

commit v3 on v2

--- a/solution.py
+++ b/solution.py
@@ -142,7 +142,7 @@
                     (((1,), (1,)), ((), ())), preferred_element_type=jnp.float32,
                 )
                 total = product if total is None else total + product
-            return total
+            return total * scale
 
         gram_out[chunk] = rows_of(1 - core)
         gram_part(chunk).start()
@@ -175,15 +175,19 @@
 
     def middle(step, carry):
         fetch(step, 0).wait()
-        each(lambda j: combine(step, j, False, False))
+        fetch(step + 1, 1).wait()
+
+        def both(j):
+            combine(step, j, False, False)
+            relay(step + 1, j, True)
+
+        each(both)
 
         @pl.when(step + 2 < chips)
         def _fetch():
             fetch(step + 2, 1).start()
             fetch(step + 2, 0).start()
 
-        fetch(step + 1, 1).wait()
-        each(lambda j: relay(step + 1, j, True))
         return carry
 
     lax.fori_loop(1, chips - 1, middle, 0)
@@ -191,29 +195,41 @@
     each(lambda j: combine(chips - 1, j, False, True))
     multiply(place)
 
-    def gathered(step, _):
-        def one(j, _):
+    def finish(chunk):
+        gram_part(chunk).wait_recv()
+        columns = pl.ds(pl.multiple_of(chip_at(chunk) * rows, rows), rows)
+        gram[:, columns] += gram_in[chunk]
+
+    def gathered(step, carry):
+        def arrive(j):
             gather_arrival(step - 1, j).wait_recv()
 
             @pl.when(step < chips - 1)
             def _pass_on():
                 gather_hop(step, j).start()
 
-            return _
-
-        lax.fori_loop(0, own_planes, one, 0)
+        each(arrive)
         multiply(wrap(place - way * step))
-        return _
+
+        @pl.when(step == chips // 2)
+        def _first():
+            finish(place)
+
+        @pl.when(step > chips // 2)
+        def _met():
+            finish(wrap(place - way * step))
+            finish(wrap(place - way * (chips - step + 1)))
+
+        return carry
 
     lax.fori_loop(1, chips, gathered, 0)
-
-    def finish(chunk, _):
-        gram_part(chunk).wait()
-        columns = pl.ds(pl.multiple_of(chip_at(chunk) * rows, rows), rows)
-        gram[:, columns] = (gram[:, columns] + gram_in[chunk]) * scale
-        return _
-
-    lax.fori_loop(0, chips, finish, 0)
+    finish(wrap(place - way))
+
+    def drain_gram(chunk, carry):
+        gram_part(chunk).wait_send()
+        return carry
+
+    lax.fori_loop(0, chips, drain_gram, 0)
 
     def drain(j, _):
         to_sibling(chips - 2, j).wait_send()
@@ -248,7 +264,7 @@
     dma = pltpu.SemaphoreType.DMA
     return pl.pallas_call(
         functools.partial(kernel, chips, lanes, 1.0 / float(planes * ranks)),
-        out_shape=jax.ShapeDtypeStruct((total_rows // devices, total_rows), f32),
+        out_shape=pltpu.VMEM((total_rows // devices, total_rows), f32),
         in_specs=[pl.BlockSpec(memory_space=pl.ANY), pl.BlockSpec(memory_space=pltpu.VMEM)],
         out_specs=pl.BlockSpec(memory_space=pltpu.VMEM),
         scratch_shapes=[
@@ -272,7 +288,7 @@
             dma((chips,)),
         ],
         compiler_params=pltpu.CompilerParams(
-            collective_id=0, has_side_effects=True, vmem_limit_bytes=60 * 2**20
+            collective_id=0, has_side_effects=True, vmem_limit_bytes=54 * 2**20
         ),
         cost_estimate=pl.CostEstimate(
             flops=8 * planes * total_rows * depth * ranks, bytes_accessed=4 * slab.size, transcendentals=0

time: 139 us -> 134 us (0.964)
  Pallas kernels: 135 us -> 132 us
  local copies, waits for them, and re-layouts: 4.65 us -> 2.02 us
    unnamed x1, local copies, waits for them, and re-layouts: 4.65 us -> 2.02 us
    pallas_call x1, Pallas kernels: 135 us -> 132 us  [shards(): pl.pallas_call(functools.partial(kernel, chips, lanes, 1.0 / float(planes...]
where the time goes in v3:
time: 134 us
  Pallas kernels  132 us (99%)
  local copies, waits for them, and re-layouts  2.02 us (2%)
    pallas_call x1, Pallas kernels, shards(): pl.pallas_call(functools.partial(kernel, chips, lanes, 1.0 / float(planes...  132 us

profile of v3, /device:TPU:0, one launch (start us, length us, event | category | flops | bytes accessed | tf_op | source)
XLA Modules:
  0.0 134.3 jit_solution(11780848802793168843)
XLA Ops:
  0.0 132.3 %shard_map.28 = f32[256,4096]{1,0:T(8,128)S(1)} custom-call(f32[6,4096,256]{2,1,0:T(8,128)} %bitcast.1, f32[256,256]{1,0:T(8,128)} %factor.1), custom_call_target="tpu_custom_call" | custom-call | flops 12884901888 | bytes 25165824 | tf_op jit(solution)/shard_map/pallas_call | solution.py:265
  132.3 2.0 %copy.4 = f32[256,4096]{1,0:T(8,128)} copy(f32[256,4096]{1,0:T(8,128)S(1)} %shard_map.28) | data formatting | bytes 8388608

commit v4 on v3

--- a/solution.py
+++ b/solution.py
@@ -104,11 +104,14 @@
         dot = functools.partial(jnp.dot, preferred_element_type=jnp.float32)
         return dot(high, fsplit[0]) + (dot(high, fsplit[1]) + dot(low, fsplit[0]))
 
+    def prepare(step, j):
+        slot = lax.rem(step, 2)
+        stage[slot, j] = term(slot, 1, j)
+
     def relay(step, j, reuse):
-        slot = lax.rem(step, 2)
         if reuse:
             to_sibling(step - 2, j).wait_send()
-        stage[slot, j] = term(slot, 1, j)
+        prepare(step, j)
         to_sibling(step, j).start()
 
     def combine(step, j, first, last):
@@ -159,15 +162,13 @@
     barrier = pltpu.get_barrier_semaphore()
     for other in (after, before, sibling):
         pl.semaphore_signal(barrier, inc=1, device_id=other, device_id_type=pl.DeviceIdType.MESH)
+    fetch(0, 1).wait()
+    each(lambda j: prepare(0, j))
     pl.semaphore_wait(barrier, 3)
 
-    fetch(0, 1).wait()
-    relay(0, 0, False)
+    each(lambda j: to_sibling(0, j).start())
     fetch(0, 0).wait()
-    for j in range(own_planes):
-        if j + 1 < own_planes:
-            relay(0, j + 1, False)
-        combine(0, j, True, False)
+    each(lambda j: combine(0, j, True, False))
     fetch(2, 1).start()
     fetch(2, 0).start()
     fetch(1, 1).wait()

time: 134 us -> 135 us (level)
  no operation moved by 1% of the time
where the time goes in v4:
time: 135 us
  Pallas kernels  133 us (99%)
  local copies, waits for them, and re-layouts  2.02 us (1%)
    pallas_call x1, Pallas kernels, shards(): pl.pallas_call(functools.partial(kernel, chips, lanes, 1.0 / float(planes...  133 us

profile of v4, /device:TPU:0, one launch (start us, length us, event | category | flops | bytes accessed | tf_op | source)
XLA Modules:
  0.0 134.8 jit_solution(14281517229923201654)
XLA Ops:
  0.0 132.8 %shard_map.28 = f32[256,4096]{1,0:T(8,128)S(1)} custom-call(f32[6,4096,256]{2,1,0:T(8,128)} %bitcast.1, f32[256,256]{1,0:T(8,128)} %factor.1), custom_call_target="tpu_custom_call" | custom-call | flops 12884901888 | bytes 25165824 | tf_op jit(solution)/shard_map/pallas_call | solution.py:266
  132.8 2.0 %copy.4 = f32[256,4096]{1,0:T(8,128)} copy(f32[256,4096]{1,0:T(8,128)S(1)} %shard_map.28) | data formatting | bytes 8388608

commit v5 on v3

--- a/solution.py
+++ b/solution.py
@@ -149,9 +149,8 @@
         columns = pl.ds(pl.multiple_of(chip_at(chunk) * rows, rows), rows)
         gram[:, columns] = rows_of(core)
 
-    for step in range(2):
-        fetch(step, 1).start()
-        fetch(step, 0).start()
+    fetch(0, 1).start()
+    fetch(0, 0).start()
     f = factor[...]
     fsplit[0] = f.astype(jnp.bfloat16)
     fsplit[1] = (f - f.astype(jnp.bfloat16).astype(jnp.float32)).astype(jnp.bfloat16)
@@ -164,6 +163,8 @@
     fetch(0, 1).wait()
     relay(0, 0, False)
     fetch(0, 0).wait()
+    fetch(1, 1).start()
+    fetch(1, 0).start()
     for j in range(own_planes):
         if j + 1 < own_planes:
             relay(0, j + 1, False)

time: 134 us -> 134 us (level)
  no operation moved by 1% of the time
where the time goes in v5:
time: 134 us
  Pallas kernels  132 us (99%)
  local copies, waits for them, and re-layouts  2.02 us (2%)
    pallas_call x1, Pallas kernels, shards(): pl.pallas_call(functools.partial(kernel, chips, lanes, 1.0 / float(planes...  132 us

profile of v5, /device:TPU:0, one launch (start us, length us, event | category | flops | bytes accessed | tf_op | source)
XLA Modules:
  0.0 134.3 jit_solution(15344233266142193823)
XLA Ops:
  0.0 132.3 %shard_map.28 = f32[256,4096]{1,0:T(8,128)S(1)} custom-call(f32[6,4096,256]{2,1,0:T(8,128)} %bitcast.1, f32[256,256]{1,0:T(8,128)} %factor.1), custom_call_target="tpu_custom_call" | custom-call | flops 12884901888 | bytes 25165824 | tf_op jit(solution)/shard_map/pallas_call | solution.py:266
  132.3 2.0 %copy.4 = f32[256,4096]{1,0:T(8,128)} copy(f32[256,4096]{1,0:T(8,128)S(1)} %shard_map.28) | data formatting | bytes 8388608
